TPU v7x, 512 devices: a whole 4x8x8 slice. The times are simulated.
512 devices in a mesh: dp: 16 (over y, z_hi), fsdp: 32 (over x, z_lo, core).
Axes of the slice: x: 4, y: 8, z: 8 (z_hi: 2, z_lo: 4; z = z_hi * 4 + z_lo), core: 2. Of those that a mesh axis runs over, the one named last changes fastest.
Arguments:
- tokens: bfloat16 [65536, 8192], P(('dp', 'fsdp')), may hold values from -6 to 6
- grad_out: bfloat16 [65536, 512], P(('dp', 'fsdp')), may hold values from -6 to 6
- base_weight: bfloat16 [8192, 512], P('fsdp'), may hold values from -0.0625 to 0.0625
- frozen_down: bfloat16 [16, 8192, 128], P('dp', 'fsdp'), may hold values from -0.0625 to 0.0625
- trained_up: bfloat16 [16, 128, 512], P('dp', None, 'fsdp'), may hold values from -0.5 to 0.5
- tenant_per_group: int32 [16], P('dp'), may hold values from 0 to 15, as said below
- lengths: int32 [16, 32], P('dp', 'fsdp'), may hold values from 32 to 128, as said below
- ranks: int32 [16], replicated, may hold values from 16 to 128, as said below
Outputs:
- projected: bfloat16 [65536, 512], P(('dp', 'fsdp'))
- input_token_gradient: bfloat16 [65536, 8192], P(('dp', 'fsdp'))
- tenant_up_gradient: float32 [16, 128, 512], P('dp', None, 'fsdp')
Inputs may be any that keep to these rules, and one draw needn't show every extreme that they name: `tenant_per_group`: exactly one tenant runs on two indices of dp, exactly one on none, every other on one; some index g of dp runs tenant g - 1 (counted round). `lengths`: at least 32 on every device; some device is full in every draw. `ranks`: multiples of 16; some tenant has the largest rank in every draw.
All inputs are finite; a program needn't handle non-finite values.
Results may differ from a plain program's by a relative error of at most 0.003.
Values may be sent and summed in bfloat16 or wider, within the bound.
A program may use at most 64 MiB of HBM per device.

v0:
```python
import jax
import jax.numpy as jnp
from jax import lax
from jax.sharding import PartitionSpec as P

adapter_alpha_factor = 2.0


def per_device(
    tokens, grad_out, base_weight, frozen_down, trained_up, tenant_per_group, lengths, ranks
):
    tok_rows = tokens.shape[0]
    tenant = tenant_per_group[0]
    count = lengths[0, 0]
    adapter_rank = ranks[tenant]
    adapter_scale = adapter_alpha_factor / jnp.sqrt(adapter_rank.astype(jnp.float32))
    rank_live = (jnp.arange(frozen_down.shape[2]) < adapter_rank)[None, :]
    row_live = (jnp.arange(tok_rows) < count)[:, None]
    masked = jnp.where(row_live, grad_out, jnp.zeros_like(grad_out))
    all_down, all_up = (
        lax.all_gather(frozen_down, "dp", axis=0, tiled=True),
        lax.all_gather(trained_up, "dp", axis=0, tiled=True),
    )
    down_rows = lax.dynamic_index_in_dim(all_down, tenant, 0, keepdims=False)
    up_part = lax.dynamic_index_in_dim(all_up, tenant, 0, keepdims=False)
    upper = lax.all_gather(up_part, "fsdp", axis=1, tiled=True)
    glow = adapter_scale * lax.dot_general(
        masked, upper, (((1,), (1,)), ((), ())), preferred_element_type=jnp.float32
    )
    glow = jnp.where(rank_live, glow, 0.0).astype(jnp.bfloat16)
    full_down = lax.all_gather(down_rows, "fsdp", axis=0, tiled=True)
    low_sum = jnp.dot(tokens, full_down, preferred_element_type=jnp.float32)
    piece_weight = lax.all_gather(base_weight, "fsdp", axis=0, tiled=True)
    base_sum = jnp.dot(tokens, piece_weight, preferred_element_type=jnp.float32)
    block = lax.dot_general(
        masked, piece_weight, (((1,), (1,)), ((), ())), preferred_element_type=jnp.float32
    )
    block = (
        block
        + lax.dot_general(
            glow, full_down, (((1,), (1,)), ((), ())), preferred_element_type=jnp.float32
        )
    ).astype(jnp.bfloat16)
    base_sum, grad_x = (base_sum, block)
    low = jnp.where(rank_live, low_sum, 0.0).astype(jnp.bfloat16)
    projected = base_sum + adapter_scale * jnp.dot(low, upper, preferred_element_type=jnp.float32)
    projected = jnp.where(row_live, projected, 0.0).astype(jnp.bfloat16)
    partial_up = adapter_scale * lax.dot_general(
        low, masked, (((0,), (0,)), ((), ())), preferred_element_type=jnp.float32
    )
    tenants_all = ranks.shape[0]
    chosen = (jnp.arange(tenants_all) == tenant).astype(jnp.float32)
    group_sum = lax.psum_scatter(partial_up, "fsdp", scatter_dimension=1, tiled=True)
    spread = chosen[:, None, None] * group_sum[None, :, :]
    tenant_up_gradient = lax.psum_scatter(spread, "dp", scatter_dimension=0, tiled=True)
    return (projected, grad_x, tenant_up_gradient)


def solution(mesh):
    placed = (
        P(("dp", "fsdp"), None),
        P(("dp", "fsdp"), None),
        P("fsdp", None),
        P("dp", "fsdp", None),
        P("dp", None, "fsdp"),
        P("dp"),
        P("dp", "fsdp"),
        P(),
    )
    return jax.shard_map(
        per_device,
        mesh=mesh,
        in_specs=placed,
        out_specs=(P(("dp", "fsdp"), None), P(("dp", "fsdp"), None), P("dp", None, "fsdp")),
        check_vma=False,
    )
```

profile of v0, /device:TPU:1, one launch (start us, length us, event | category | flops | bytes accessed | tf_op | source)
XLA Modules:
  0.0 612.6 jit_solution(3310726649726855240)
XLA Ops:
  7.2 0.7 all-gather.8.cloned.1.call-update
  7.9 0.0 all-gather.10.cloned.1.call-start
  8.6 97.4 %all-gather.8.cloned.1.call-done = bf16[16,256,128]{2,1,0:T(8,128)(2,1)} async-done(((bf16[1,256,128]{2,1,0:T(8,128)(2,1)}), bf16[16,256,128]{2,1,0:T(8,128)(2,1)}) %all-gather.8.cloned.1.call-update) | async-done | bytes 1048592 | tf_op jit(solution)/shard_map/all_gather | solution.py:21
  106.0 1.5 constant_dynamic-slice_fusion.1
  107.5 0.0 reduce-scatter.7.cloned.1.call-start
  107.5 1.2 dynamic_slice.11
  110.1 0.7 iota_compare_fusion
  110.8 59.3 %all-gather.10.cloned.1.call-done = bf16[1,8192,128]{2,1,0:T(8,128)(2,1)} async-done(((bf16[1,256,128]{2,1,0:T(8,128)(2,1)}), bf16[1,8192,128]{2,1,0:T(8,128)(2,1)}) %all-gather.10.cloned.1.call-update) | async-done | bytes 2097168 | tf_op jit(solution)/shard_map/all_gather | solution.py:31
  170.0 2.4 fusion.11
  172.4 0.2 convolution_multiply_fusion
  172.7 0.8 copy.16
  173.5 0.0 all-gather.6.cloned.1.call-start
  173.6 0.5 all-gather.6.cloned.1.call-update
  174.2 44.8 %all_gather.18 = bf16[16,128,16]{1,2,0:T(8,128)(2,1)S(1)} all-gather(bf16[1,128,16]{1,2,0:T(8,128)(2,1)S(1)} %copy-done.3), channel_id=1, replica_groups=mesh['dp'=16,'fsdp'=32] {'dp'}, dimensions={0}, use_global_device_ids=true | all-gather | bytes 69632 | tf_op jit(solution)/shard_map/all_gather | solution.py:22
  219.0 48.3 %all-gather.1 = bf16[1,128,512]{1,2,0:T(8,128)(2,1)S(1)} all-gather(bf16[1,128,16]{1,2,0:T(8,128)(2,1)S(1)} %constant_dynamic-slice_fusion), channel_id=3, replica_groups=mesh['dp'=16,'fsdp'=32] {'fsdp'}, dimensions={2}, use_global_device_ids=true | all-gather | bytes 135168 | tf_op jit(solution)/shard_map/all_gather | solution.py:26
  267.3 47.2 %reduce-scatter.7.cloned.1.call-done = f32[16,128]{1,0:T(8,128)} async-done(((f32[512,128]{1,0:T(8,128)}), f32[16,128]{1,0:T(8,128)}) %reduce-scatter.7.cloned.1.call-update) | async-done | bytes 8208
  314.6 1.4 broadcast_multiply_fusion
  316.0 73.9 %all-gather.6.cloned.1.call-done = bf16[8192,512]{1,0:T(8,128)(2,1)} async-done(((bf16[256,512]{1,0:T(8,128)(2,1)}), bf16[8192,512]{1,0:T(8,128)(2,1)}) %all-gather.6.cloned.1.call-update) | async-done | bytes 8388624 | tf_op jit(solution)/shard_map/all_gather | solution.py:33
  389.9 4.8 fusion.23
  394.7 1.0 copy-done.1
  395.7 4.8 fusion.22
  400.5 5.0 fusion
  405.5 0.9 fusion.6
  406.4 199.7 %reduce-scatter.5.cloned.1.call-done = f32[1,128,16]{1,2,0:T(8,128)} async-done(((f32[16,128,16]{1,2,0:T(8,128)}), f32[1,128,16]{1,2,0:T(8,128)}) %reduce-scatter.5.cloned.1.call-update) | async-done | bytes 8208 | tf_op jit(solution)/shard_map/reduce_scatter | solution.py:55
  (14 shorter events, 0.1 us)
Async XLA Ops:
  7.2 162.9 %copy-start = (bf16[128,8192]{1,0:T(8,128)(2,1)S(1)}, bf16[128,8192]{1,0:T(8,128)(2,1)}, u32[]{:S(2)}) copy-start(bf16[128,8192]{1,0:T(8,128)(2,1)} %param.8) | copy-start | bytes 6291460
  7.2 98.8 %all-gather.8.cloned.1.call-start = ((), (), s32[]{:S(2)}) async-start(), calls=%async_computation.3 | async-start | bytes 1114112 | tf_op jit(solution)/shard_map/all_gather | solution.py:21
  7.9 162.1 %all-gather.10.cloned.1.call-start = ((), (), s32[]{:S(2)}) async-start(), calls=%async_computation.5 | async-start | bytes 2162688 | tf_op jit(solution)/shard_map/all_gather | solution.py:31
  107.5 207.1 %reduce-scatter.7.cloned.1.call-start = ((), (), s32[]{:S(2)}) async-start(), calls=%async_computation.6 | async-start | bytes 270336
  170.0 2.4 copy-start.2
  170.0 4.1 copy-start.3
  173.5 216.4 %all-gather.6.cloned.1.call-start = ((), (), s32[]{:S(2)}) async-start(), calls=%async_computation.2 | async-start | bytes 8650752 | tf_op jit(solution)/shard_map/all_gather | solution.py:33
  174.1 431.9 %reduce-scatter.5.cloned.1.call-start = ((), (), s32[]{:S(2)}) async-start(), calls=%async_computation.4 | async-start | bytes 139264 | tf_op jit(solution)/shard_map/reduce_scatter | solution.py:55
  389.9 5.8 copy-start.1
Sparse Core Ops, SparseCore 0:
  11.2 94.7 all-gather.7
  108.7 61.2 all-gather.9
  173.7 140.8 reduce-scatter.6
  316.8 73.0 all-gather.5
  395.4 210.6 reduce-scatter.4
where the time goes:
time: 617 us; the launch traced here: 613 us
  waiting for transfers between devices  479 us (78%)
  blocking collectives  93.2 us (15%)
  matrix products  18.1 us (3%)
  between operations  15.8 us (3%)
    reduce_scatter x1, waiting for transfers between devices, per_device(): lax.psum_scatter(spread, 'dp', scatter_dimension=0, tiled=True)  200 us
    all_gather x1, waiting for transfers between devices, per_device(): lax.all_gather(frozen_down, 'dp', axis=0, tiled=True)  97.4 us
    all_gather x1, waiting for transfers between devices, per_device(): piece_weight = lax.all_gather(base_weight, 'fsdp', axis=0, tiled=True)  73.9 us
    all_gather x1, waiting for transfers between devices, per_device(): full_down = lax.all_gather(down_rows, 'fsdp', axis=0, tiled=True)  59.3 us
    unnamed x6, waiting for transfers between devices  48.5 us
    all_gather x1, blocking collectives, per_device(): upper = lax.all_gather(up_part, 'fsdp', axis=1, tiled=True)  48.3 us
    all_gather x1, blocking collectives, per_device(): lax.all_gather(trained_up, 'dp', axis=0, tiled=True)  44.8 us
  transfers between devices with their start and end apart: 5, of which 5 were waited for; matrix products, arithmetic and copies ran while one was open for 3% of the time, Pallas kernels for 0%

commit v1 on v0

v1 whole, which is shorter than its diff:
```python
import functools

import jax
import jax.numpy as jnp
from jax import lax
from jax.experimental import pallas as pl
from jax.experimental.pallas import tpu as pltpu
from jax.sharding import PartitionSpec as P

adapter_alpha_factor = 2.0

MESH = pl.DeviceIdType.MESH
BF, F32 = jnp.bfloat16, jnp.float32

NX = 4
NZL = 4
NZ = 8
N_FSDP = 32
RW = 256
VW = 512
R = 128
TOK = 128
CB = VW // N_FSDP
AR = RW + CB
AH = 144
H1 = 128
PARTS = ((0, H1, H1 // 2), (H1, RW, H1 + (RW - H1) // 2))
REL = (0, 1, 3, 2)


def dot_nn(a, b):
    return lax.dot_general(a, b, (((1,), (0,)), ((), ())), preferred_element_type=F32)


def dot_nt(a, b):
    return lax.dot_general(a, b, (((1,), (1,)), ((), ())), preferred_element_type=F32)


def kernel(
    n_dp, tok_hbm, grad_hbm, w_hbm, a_hbm, bt_hbm, tid_s, len_s, rank_s,
    proj_ref, gx_ref, gup_ref,
    tok, masked, glow, w, a, a_own, bt_own, m_out, m_in, q_out, bt, rs_out, rs_in, dp_out, dp_in,
    proj_acc, low_acc,
    load_sem, sw_ici, sw_d2d, sa_ici, sa_d2d, s_hop, rw_ici, rw_d2d, ra_z, ra_x, ra_dz, ra_dx, r_hop,
):
    pr = RW // n_dp
    g = lax.axis_index("dp")
    f = lax.axis_index("fsdp")
    y, zh = g // 2, g % 2
    x, zl, c = f // 8, (f // 2) % 4, f % 2
    z = zh * NZL + zl

    def at(dx, dz):
        xx, zz = (x + dx) % NX, (z + dz) % NZ
        return (y * 2 + zz // NZL, xx * 8 + (zz % NZL) * 2 + c)

    partner = (g, f + 1 - 2 * c)
    x_up, x_dn = at(1, 0), at(NX - 1, 0)
    z_up, z_dn = at(0, 1), at(0, NZ - 1)

    loads = [
        pltpu.make_async_copy(w_hbm, w.at[pl.ds(pl.multiple_of(f * RW, RW), RW)], load_sem.at[0]),
        pltpu.make_async_copy(a_hbm, a_own, load_sem.at[1]),
        pltpu.make_async_copy(bt_hbm, bt_own, load_sem.at[2]),
        pltpu.make_async_copy(grad_hbm, masked, load_sem.at[3]),
        pltpu.make_async_copy(tok_hbm, tok, load_sem.at[4]),
    ]
    for load in loads:
        load.start()

    barrier = pltpu.get_barrier_semaphore()

    def greet(dev):
        pl.semaphore_signal(barrier, inc=1, device_id=dev, device_id_type=MESH)

    greet(z_up)
    greet(z_dn)

    def greet_fsdp(k, _):
        greet((g, (f + k) % N_FSDP))
        return 0

    def greet_dp(k, _):
        greet(((g + k) % n_dp, f))
        return 0

    lax.fori_loop(1, N_FSDP, greet_fsdp, 0)
    lax.fori_loop(1, n_dp, greet_dp, 0)

    loads[1].wait()
    loads[2].wait()
    tenant = tid_s[0]
    rank = rank_s[tenant]
    tid_tile = jnp.full((16, R), tenant, jnp.int32).astype(F32).astype(BF)

    def pack(j, _):
        m_out[j, 0:pr] = a_own[pl.ds(pl.multiple_of(j * pr, pr), pr)]
        m_out[j, pr : pr + CB] = bt_own[...]
        m_out[j, pr + CB : pr + CB + 16] = tid_tile
        return 0

    lax.fori_loop(0, n_dp, pack, 0)
    m_in[g] = m_out[g]

    scale = adapter_alpha_factor / jnp.sqrt(jnp.full((1, R), rank, jnp.int32).astype(F32))
    scale_wide = adapter_alpha_factor / jnp.sqrt(jnp.full((1, VW), rank, jnp.int32).astype(F32))
    rank_live = lax.broadcasted_iota(jnp.int32, (TOK, R), 1) < rank
    row_live = lax.broadcasted_iota(jnp.int32, (TOK, VW), 0) < len_s[0, 0]
    loads[3].wait()
    masked[...] = jnp.where(row_live, masked[...].astype(F32), 0.0).astype(BF)
    proj_acc[...] = jnp.zeros_like(proj_acc)
    low_acc[...] = jnp.zeros_like(low_acc)
    loads[0].wait()
    pl.semaphore_wait(barrier, N_FSDP - 1 + n_dp - 1 + 2)

    def remote(src, dst, send, recv, dev):
        return pltpu.make_async_remote_copy(
            src_ref=src, dst_ref=dst, send_sem=send, recv_sem=recv, device_id=dev, device_id_type=MESH
        )

    def arrived(ref, sem):
        remote(ref, ref, s_hop.at[0], sem, partner).wait_recv()

    def sent(ref, sem):
        remote(ref, ref, sem, r_hop.at[0], partner).wait_send()

    def hop1(k, _):
        j = (g + k) % n_dp
        remote(m_out.at[j], m_in.at[g], s_hop.at[0], r_hop.at[0], (j, f)).start()
        return 0

    lax.fori_loop(1, n_dp, hop1, 0)

    def place(dx, dz):
        return ((x + dx) % NX) * 8 + ((zl + dz) % NZL) * 2 + c

    def w_rows(dx, dz, lo, hi):
        return w.at[pl.ds(pl.multiple_of(place(dx, dz) * RW + lo, 16), hi - lo)]

    def span(stream, part):
        lo, hi, mid = PARTS[stream]
        return {"all": (lo, hi), "lo": (lo, mid), "hi": (mid, hi)}[part]

    def slot(dx, dz):
        return (dx % 4) * 4 + dz % 4

    def w_send(stream, dx, dz, part, axis, step):
        ref = w_rows(dx, dz, *span(stream, part))
        if axis == "x":
            dev = x_up if step == 1 else x_dn
            there = slot(dx - step, dz)
        else:
            dev = z_up if step == 1 else z_dn
            there = slot(dx, dz - step)
        remote(ref, ref, sw_ici, rw_ici.at[stream, there, int(part == "hi")], dev).start()

    def w_d2d(stream, dx, dz, part):
        ref = w_rows(dx, dz, *span(stream, part))
        remote(ref, ref, sw_d2d, rw_d2d.at[stream, slot(dx, dz), int(part == "hi")], partner).start()

    def w_wait(stream, dx, dz, part):
        arrived(w_rows(dx, dz, *span(stream, part)), rw_ici.at[stream, slot(dx, dz), int(part == "hi")])
        w_d2d(stream, dx, dz, part)

    def other_rows(dx, dz, lo, hi):
        return w.at[pl.ds(pl.multiple_of((place(dx, dz) + 1 - 2 * c) * RW + lo, 16), hi - lo)]

    def w_other(dx, dz):
        for stream in (0, 1):
            for part in parts_of(stream, dx, dz):
                arrived(other_rows(dx, dz, *span(stream, part)), rw_d2d.at[stream, slot(dx, dz), int(part == "hi")])

    def parts_of(stream, dx, dz):
        last = 0
        if stream == 0:
            last = dz if dz else dx
        else:
            last = dx if dx else dz
        return ("lo", "hi") if last == 2 else ("all",)

    def pick(stream, p, q):
        return (p, q) if stream == 0 else (q, p)

    axes = (("x", "z"), ("z", "x"))

    def first_start():
        for stream in (0, 1):
            for step in (1, -1):
                w_send(stream, 0, 0, "all", axes[stream][0], step)
        for stream in (0, 1):
            w_d2d(stream, 0, 0, "all")

    def second_start(p):
        for stream in (0, 1):
            for step in (1, -1):
                w_send(stream, *pick(stream, p, 0), "all", axes[stream][1], step)

    def first_wait(p):
        for stream in (0, 1):
            if p == 2:
                for part in ("lo", "hi"):
                    w_wait(stream, *pick(stream, p, 0), part)
            else:
                w_wait(stream, *pick(stream, p, 0), "all")
                if p == 3:
                    w_send(stream, *pick(stream, p, 0), "lo", axes[stream][0], 1)
                else:
                    w_send(stream, *pick(stream, p, 0), "hi", axes[stream][0], -1)

    def second_wait(p):
        for stream in (0, 1):
            for q in (3, 1):
                w_wait(stream, *pick(stream, p, q), "all")
                if q == 3:
                    w_send(stream, *pick(stream, p, q), "lo", axes[stream][1], 1)
                else:
                    w_send(stream, *pick(stream, p, q), "hi", axes[stream][1], -1)

    def last_wait(p):
        for stream in (0, 1):
            for part in ("lo", "hi"):
                w_wait(stream, *pick(stream, p, 2), part)

    def choose(tile, first, rows):
        total = jnp.zeros((rows, R), F32)
        for u in range(n_dp):
            total = total + jnp.where(tile == u, m_in[u, first : first + rows].astype(F32), 0.0)
        return total.astype(BF)

    def tile_of(k, rows):
        t = m_in[k, pr + CB : pr + CB + 16].astype(F32)
        return jnp.broadcast_to(t[0:1], (rows, R)) if rows != 16 else t

    def second_hop():
        arrived(m_in.at[pl.ds(0, n_dp - 1)], r_hop.at[0])

        def hop2(k, _):
            j = (g + k) % n_dp
            q_out[j] = choose(tile_of(j, pr), 0, pr)
            mine = a.at[f, pl.ds(pl.multiple_of(g * pr, pr), pr)]
            remote(q_out.at[j], mine, s_hop.at[1], r_hop.at[1], (j, f)).start()
            return 0

        lax.fori_loop(1, n_dp, hop2, 0)
        a[f, pl.ds(pl.multiple_of(g * pr, pr), pr)] = choose(tile_of(g, pr), 0, pr)
        a[f, RW:AR] = choose(tile_of(g, CB), pr, CB)

    def z_near(s):
        return (zl, zl + 1 - 2 * (zl % 2), zl + 2 - 4 * (zl // 2), 3 - zl)[s]

    def a_slot(dx, s):
        return ((x + dx) % NX) * 8 + z_near(s) * 2 + c

    def a_other(dx, s):
        return a_slot(dx, s) + 1 - 2 * c

    def a_d2d(ref, sem):
        remote(ref, ref, sa_d2d, sem, partner).start()

    def a_start():
        arrived(a.at[f, pl.ds(0, (n_dp - 1) * pr)], r_hop.at[1])
        ref = a.at[f]
        for s in (1, 2, 3):
            remote(ref, ref, sa_ici, ra_z.at[s], (g, a_slot(0, s))).start()
        a_d2d(ref, ra_dz.at[0])
        a_along_x(0)

    def a_along_x(s):
        ref = a.at[a_slot(0, s)]
        remote(ref, ref, sa_ici, ra_x.at[s, 0], x_up).start()
        remote(ref, ref, sa_ici, ra_x.at[s, 1], x_dn).start()

    def a_z_wait(s):
        ref = a.at[a_slot(0, s)]
        arrived(ref, ra_z.at[s])
        a_d2d(ref, ra_dz.at[s])
        a_along_x(s)

    def a_x_wait(s):
        dn = a.at[a_slot(3, s)]
        arrived(dn, ra_x.at[s, 0])
        part = a.at[a_slot(3, s), pl.ds(0, AH)]
        remote(part, part, sa_ici, ra_x.at[s, 2], x_up).start()
        a_d2d(dn, ra_dx.at[s, 0])
        up = a.at[a_slot(1, s)]
        arrived(up, ra_x.at[s, 1])
        part = a.at[a_slot(1, s), pl.ds(AH, AR - AH)]
        remote(part, part, sa_ici, ra_x.at[s, 3], x_dn).start()
        a_d2d(up, ra_dx.at[s, 1])

    def a_x_last(s):
        lo = a.at[a_slot(2, s), pl.ds(0, AH)]
        arrived(lo, ra_x.at[s, 2])
        a_d2d(lo, ra_dx.at[s, 2])
        hi = a.at[a_slot(2, s), pl.ds(AH, AR - AH)]
        arrived(hi, ra_x.at[s, 3])
        a_d2d(hi, ra_dx.at[s, 3])

    def a_others():
        for s in range(4):
            arrived(a.at[a_other(0, s)], ra_dz.at[s])
            arrived(a.at[a_other(3, s)], ra_dx.at[s, 0])
            arrived(a.at[a_other(1, s)], ra_dx.at[s, 1])
            arrived(a.at[a_other(2, s), pl.ds(0, AH)], ra_dx.at[s, 2])
            arrived(a.at[a_other(2, s), pl.ds(AH, AR - AH)], ra_dx.at[s, 3])

    def cols(p):
        return pl.ds(pl.multiple_of(p * 2 * RW, 2 * RW), 2 * RW)

    def forward(p):
        proj_acc[...] += dot_nn(tok[:, cols(p)], w[cols(p)])

    def backward(p):
        base = dot_nt(masked[...], w[cols(p)])
        low_part = jnp.concatenate([dot_nt(glow[...], a[2 * p + k, 0:RW]) for k in (0, 1)], axis=1)
        gx_ref[:, cols(p)] = (base + low_part).astype(BF)

    def over(pairs, body):
        code_x = sum((dx % 4) * 4**i for i, (dx, dz) in enumerate(pairs))
        code_z = sum((dz % 4) * 4**i for i, (dx, dz) in enumerate(pairs))

        def step(_, carry):
            cx, cz = carry
            body(((x + cx % 4) % NX) * 4 + (zl + cz % 4) % NZL)
            return cx // 4, cz // 4

        lax.fori_loop(0, len(pairs), step, (jnp.int32(code_x), jnp.int32(code_z)))

    def others(pairs):
        for dx, dz in pairs:
            w_other(dx, dz)

    def both(p):
        forward(p)
        backward(p)

    first_start()
    second_hop()
    second_start(0)
    first_wait(3)
    first_wait(1)
    a_start()
    second_start(3)
    second_start(1)
    first_wait(2)
    second_start(2)
    for s in (1, 2, 3):
        a_z_wait(s)
    loads[4].wait()
    group = [(0, 0)]
    others(group)
    over(group, forward)
    second_wait(0)
    for s in range(4):
        a_x_wait(s)
    early = [(1, 0), (3, 0), (0, 1), (0, 3)]
    others(early)
    over(early, forward)
    for s in range(4):
        a_x_last(s)
    second_wait(3)
    a_others()

    for k in range(N_FSDP):
        bt[k * CB : (k + 1) * CB] = a[k, RW:AR]
    glow[...] = jnp.where(rank_live, scale * dot_nn(masked[...], bt[...]), 0.0).astype(BF)

    def low_step(k, _):
        low_acc[...] += dot_nn(tok[:, pl.ds(pl.multiple_of(k * RW, RW), RW)], a[k, 0:RW])
        return 0

    lax.fori_loop(0, N_FSDP, low_step, 0)
    low = jnp.where(rank_live, low_acc[...], 0.0).astype(BF)
    rs_out[...] = (
        lax.dot_general(masked[...], low, (((0,), (0,)), ((), ())), preferred_element_type=F32) * scale
    ).reshape(N_FSDP, CB, R)
    rs_in[f] = rs_out[f]

    def scatter(k, _):
        j = (f + k) % N_FSDP
        remote(rs_out.at[j], rs_in.at[f], s_hop.at[2], r_hop.at[2], (g, j)).start()
        return 0

    lax.fori_loop(1, N_FSDP, scatter, 0)
    proj_acc[...] += scale_wide * dot_nt(low, bt[...])

    second_wait(1)
    second_wait(2)
    over([(0, 0)] + early, backward)
    middle = [(1, 1), (1, 3), (3, 1), (3, 3)]
    others(middle)
    over(middle, both)

    arrived(rs_in.at[pl.ds(0, N_FSDP - 1)], r_hop.at[2])
    total = rs_in[0]
    for k in range(1, N_FSDP):
        total = total + rs_in[k]
    dp_out[...] = total
    dp_in[g] = total

    def spread(k, _):
        remote(dp_out, dp_in.at[g], s_hop.at[3], r_hop.at[3], ((g + k) % n_dp, f)).start()
        return 0

    lax.fori_loop(1, n_dp, spread, 0)

    last_wait(0)
    last_wait(3)
    last_wait(1)
    late = [(2, 0), (0, 2), (2, 1), (1, 2), (2, 3), (3, 2)]
    others(late)
    over(late, both)
    last_wait(2)
    others([(2, 2)])
    over([(2, 2)], both)
    proj_ref[...] = jnp.where(row_live, proj_acc[...], 0.0).astype(BF)

    arrived(dp_in.at[pl.ds(0, n_dp - 1)], r_hop.at[3])
    total = jnp.zeros((CB, R), F32)
    for k in range(n_dp):
        total = total + jnp.where(tile_of(k, CB) == g.astype(F32), dp_in[k], 0.0)
    gup_ref[...] = total

    sent(w.at[pl.ds(0, 15 * RW)], sw_ici)
    sent(w.at[pl.ds(0, 16 * RW)], sw_d2d)
    sent(a.at[pl.ds(0, 15)], sa_ici)
    sent(a.at[pl.ds(0, 16)], sa_d2d)
    sent(m_in.at[pl.ds(0, n_dp - 1)], s_hop.at[0])
    sent(q_out.at[pl.ds(0, n_dp - 1)], s_hop.at[1])
    sent(rs_in.at[pl.ds(0, N_FSDP - 1)], s_hop.at[2])
    sent(dp_in.at[pl.ds(0, n_dp - 1)], s_hop.at[3])


def per_device(
    tokens, grad_out, base_weight, frozen_down, trained_up, tenant_per_group, lengths, ranks
):
    n_dp = ranks.shape[0]
    pr = RW // n_dp
    hbm = pl.BlockSpec(memory_space=pl.ANY)
    smem = pl.BlockSpec(memory_space=pltpu.SMEM)
    vmem = pl.BlockSpec(memory_space=pltpu.VMEM)
    dma = pltpu.SemaphoreType.DMA
    projected, grad_x, up = pl.pallas_call(
        functools.partial(kernel, n_dp),
        out_shape=(
            jax.ShapeDtypeStruct((TOK, VW), BF),
            jax.ShapeDtypeStruct((TOK, N_FSDP * RW), BF),
            jax.ShapeDtypeStruct((CB, R), F32),
        ),
        in_specs=[hbm] * 5 + [smem] * 3,
        out_specs=(vmem, vmem, vmem),
        scratch_shapes=[
            pltpu.VMEM((TOK, N_FSDP * RW), BF),
            pltpu.VMEM((TOK, VW), BF),
            pltpu.VMEM((TOK, R), BF),
            pltpu.VMEM((N_FSDP * RW, VW), BF),
            pltpu.VMEM((N_FSDP, AR, R), BF),
            pltpu.VMEM((RW, R), BF),
            pltpu.VMEM((CB, R), BF),
            pltpu.VMEM((n_dp, pr + CB + 16, R), BF),
            pltpu.VMEM((n_dp, pr + CB + 16, R), BF),
            pltpu.VMEM((n_dp, pr, R), BF),
            pltpu.VMEM((VW, R), BF),
            pltpu.VMEM((N_FSDP, CB, R), F32),
            pltpu.VMEM((N_FSDP, CB, R), F32),
            pltpu.VMEM((CB, R), F32),
            pltpu.VMEM((n_dp, CB, R), F32),
            pltpu.VMEM((TOK, VW), F32),
            pltpu.VMEM((TOK, R), F32),
            dma((5,)),
            dma,
            dma,
            dma,
            dma,
            dma((4,)),
            dma((2, 16, 2)),
            dma((2, 16, 2)),
            dma((4,)),
            dma((4, 4)),
            dma((4,)),
            dma((4, 4)),
            dma((4,)),
        ],
        compiler_params=pltpu.CompilerParams(
            collective_id=0, has_side_effects=True, vmem_limit_bytes=40 * 1024 * 1024
        ),
        cost_estimate=pl.CostEstimate(
            flops=2 * 2 * TOK * N_FSDP * RW * (VW + R), bytes_accessed=5 * 1024 * 1024, transcendentals=0
        ),
        name="gather_and_multiply",
    )(
        tokens, grad_out, base_weight, frozen_down[0], jnp.swapaxes(trained_up[0], 0, 1),
        tenant_per_group, lengths, ranks,
    )
    return projected, grad_x, jnp.swapaxes(up, 0, 1)[None]


def solution(mesh):
    placed = (
        P(("dp", "fsdp"), None),
        P(("dp", "fsdp"), None),
        P("fsdp", None),
        P("dp", "fsdp", None),
        P("dp", None, "fsdp"),
        P("dp"),
        P("dp", "fsdp"),
        P(),
    )
    return jax.shard_map(
        per_device,
        mesh=mesh,
        in_specs=placed,
        out_specs=(P(("dp", "fsdp"), None), P(("dp", "fsdp"), None), P("dp", None, "fsdp")),
        check_vma=False,
    )
```

time: 617 us -> 89.1 us (0.14)
  waiting for transfers between devices: 479 us -> 0 us
  blocking collectives: 93.2 us -> 0 us
  Pallas kernels: 0 us -> 78.7 us
  matrix products: 18.1 us -> 0 us
  between operations: 15.8 us -> 1.95 us
    all_gather x3 -> x0, waiting for transfers between devices: 231 us -> none  [the longest x1 97.4 us: per_device(): lax.all_gather(frozen_down, 'dp', axis=0, tiled=True)]
    reduce_scatter x1 -> x0, waiting for transfers between devices: 200 us -> none  [per_device(): lax.psum_scatter(spread, 'dp', scatter_dimension=0, tiled=True)]
    all_gather x2 -> x0, blocking collectives: 93.2 us -> none  [the longest x1 48.3 us: per_device(): upper = lax.all_gather(up_part, 'fsdp', axis=1, tiled=True)]
    pallas_call x0 -> x1, Pallas kernels: none -> 78.7 us  [per_device(): pl.pallas_call(functools.partial(kernel, n_dp), out_shape=(jax.ShapeDtype...]
    unnamed x6 -> x0, waiting for transfers between devices: 48.5 us -> none
    dot_general x6 -> x0, matrix products: 18.1 us -> none  [the longest x1 5.03 us: per_device(): lax.dot_general(glow, full_down, (((1,), (1,)), ((), ())), preferred_elem...]
    unnamed x9 -> x15, local copies, waits for them, and re-layouts: 1.83 us -> 8.19 us
  transfers between devices with their start and end apart: 5 -> 0, of which waited for: 5 -> 0; matrix products, arithmetic and copies ran while one was open for 3% -> 0% of each run, Pallas kernels for 0% -> 0%
where the time goes in v1:
time: 89.1 us; the launch traced here: 88.8 us
  Pallas kernels  78.7 us (88%)
  local copies, waits for them, and re-layouts  8.19 us (9%)
  between operations  1.95 us (2%)
    pallas_call x1, Pallas kernels, per_device(): pl.pallas_call(functools.partial(kernel, n_dp), out_shape=(jax.ShapeDtype...  78.7 us
    unnamed x15, local copies, waits for them, and re-layouts  8.19 us

profile of v1, /device:TPU:1, one launch (start us, length us, event | category | flops | bytes accessed | tf_op | source)
XLA Modules:
  0.0 88.8 jit_solution(17670615264171647540)
XLA Ops:
  1.9 0.0 copy-start
  1.9 1.6 %copy-done = bf16[128,8192]{1,0:T(8,128)(2,1)S(1)} copy-done((bf16[128,8192]{1,0:T(8,128)(2,1)S(1)}, bf16[128,8192]{1,0:T(8,128)(2,1)}, u32[]{:S(2)}) %copy-start) | copy-done | bytes 2097176
  3.5 0.0 copy-start.1
  3.5 0.9 %copy-done.1 = bf16[256,512]{1,0:T(8,128)(2,1)S(1)} copy-done((bf16[256,512]{1,0:T(8,128)(2,1)S(1)}, bf16[256,512]{1,0:T(8,128)(2,1)}, u32[]{:S(2)}) %copy-start.1) | copy-done | bytes 262168
  4.5 0.0 copy-start.2
  4.5 0.9 %copy-done.2 = bf16[128,512]{1,0:T(8,128)(2,1)S(1)} copy-done((bf16[128,512]{1,0:T(8,128)(2,1)S(1)}, bf16[128,512]{1,0:T(8,128)(2,1)}, u32[]{:S(2)}) %copy-start.2) | copy-done | bytes 131096
  5.4 0.0 copy-start.3
  5.4 0.8 copy-done.3
  6.2 0.0 copy-start.4
  6.2 0.7 copy-done.4
  6.9 0.0 copy-start.5
  6.9 0.7 copy-done.5
  7.6 78.7 %gather_and_multiply.1 = (bf16[128,512]{1,0:T(8,128)(2,1)S(1)}, bf16[128,8192]{1,0:T(8,128)(2,1)S(1)}, f32[16,128]{1,0:T(8,128)S(1)}) custom-call(bf16[128,8192]{1,0:T(8,128)(2,1)S(1)} %copy-done, bf16[128,512]{1,0:T(8,128)(2,1)S(1)} %copy-done.2, bf16[256,512]{1,0:T(8,128)(2,1)S(1)} %copy-done.1, bf16[256,128]{1,0:T(8,128)(2,1)S(1)} %bitcast.8, ...), custom_call_target="tpu_custom_call" | custom-call | flops 2684354560 | bytes 5242880 | tf_op jit(solution)/shard_map/gather_and_multiply/pallas_call | solution.py:443
  86.2 0.7 copy.16
  86.9 1.3 %copy.17 = bf16[128,8192]{1,0:T(8,128)(2,1)} copy(bf16[128,8192]{1,0:T(8,128)(2,1)S(1)} %get-tuple-element.13) | data formatting | bytes 4194304
  88.2 0.6 copy.18
Async XLA Ops:
  1.9 1.6 %copy-start = (bf16[128,8192]{1,0:T(8,128)(2,1)S(1)}, bf16[128,8192]{1,0:T(8,128)(2,1)}, u32[]{:S(2)}) copy-start(bf16[128,8192]{1,0:T(8,128)(2,1)} %tok_hbm.1) | copy-start | bytes 6291460
  3.5 0.9 %copy-start.1 = (bf16[256,512]{1,0:T(8,128)(2,1)S(1)}, bf16[256,512]{1,0:T(8,128)(2,1)}, u32[]{:S(2)}) copy-start(bf16[256,512]{1,0:T(8,128)(2,1)} %w_hbm.1) | copy-start | bytes 786436
  4.5 0.9 %copy-start.2 = (bf16[128,512]{1,0:T(8,128)(2,1)S(1)}, bf16[128,512]{1,0:T(8,128)(2,1)}, u32[]{:S(2)}) copy-start(bf16[128,512]{1,0:T(8,128)(2,1)} %grad_hbm.1) | copy-start | bytes 393220
  5.4 0.8 copy-start.3
  6.2 0.7 copy-start.4
  6.9 0.7 copy-start.5

commit v2 on v1

v2 whole, which is shorter than its diff:
```python
import functools

import jax
import jax.numpy as jnp
from jax import lax
from jax.experimental import pallas as pl
from jax.experimental.pallas import tpu as pltpu
from jax.sharding import PartitionSpec as P

adapter_alpha_factor = 2.0

MESH = pl.DeviceIdType.MESH
BF, F32 = jnp.bfloat16, jnp.float32

NX = 4
NZL = 4
NZ = 8
N_FSDP = 32
RW = 256
VW = 512
R = 128
TOK = 128
N_CHIP = N_FSDP // 2
CB = VW // N_FSDP
AH = RW // 2
SIDE = 80


def dot_nn(a, b):
    return lax.dot_general(a, b, (((1,), (0,)), ((), ())), preferred_element_type=F32)


def dot_nt(a, b):
    return lax.dot_general(a, b, (((1,), (1,)), ((), ())), preferred_element_type=F32)


def kernel(
    n_dp, tok_hbm, grad_hbm, w_hbm, a_hbm, bt_hbm, tid_s, len_s, rank_s,
    proj_ref, gx_ref, gup_ref,
    tok, masked, glow, w, a, tid_all, a_in, b_in, q_out, bt_in, bt, rs_out, rs_mid, rs_in, dp_out, dp_in,
    proj_acc, low_acc,
    load_sem, sw_ici, sw_d2d, sa_ici, sa_d2d, s_hop, rw_ici, rw_d2d, ra_z, ra_x, ra_dz, ra_dx, r_hop,
):
    n_y = n_dp // 2
    pr = RW // n_y
    g = lax.axis_index("dp")
    f = lax.axis_index("fsdp")
    y, zh = g // 2, g % 2
    x, zl, c = f // 8, (f // 2) % 4, f % 2
    z = zh * NZL + zl

    def at(dx, dz):
        xx, zz = (x + dx) % NX, (z + dz) % NZ
        return (y * 2 + zz // NZL, xx * 8 + (zz % NZL) * 2 + c)

    partner = (g, f + 1 - 2 * c)
    x_up, x_dn = at(1, 0), at(NX - 1, 0)
    z_up, z_dn = at(0, 1), at(0, NZ - 1)
    y_up, y_dn = ((y + 1) % n_y * 2 + zh, f), ((y + n_y - 1) % n_y * 2 + zh, f)

    loads = [
        pltpu.make_async_copy(w_hbm, w.at[pl.ds(pl.multiple_of(f * RW, RW), RW)], load_sem.at[0]),
        pltpu.make_async_copy(a_hbm.at[pl.ds(pl.multiple_of(y * pr, pr), pr)], a_in.at[g], load_sem.at[1]),
        pltpu.make_async_copy(bt_hbm, b_in.at[g], load_sem.at[2]),
        pltpu.make_async_copy(grad_hbm, masked, load_sem.at[3]),
        pltpu.make_async_copy(tok_hbm, tok, load_sem.at[4]),
    ]

    by_distance = sorted(range(n_y), key=lambda d: -min(d, n_y - d))
    dp_peers = [((y + d) % n_y * 2 + (zh + e) % 2, f) for e in (1, 0) for d in by_distance if d or e]
    chip = f // 2

    def chip_peer(k):
        return (g, (chip + k) % N_CHIP * 2 + c)

    barrier = pltpu.get_barrier_semaphore()

    def greet(dev):
        pl.semaphore_signal(barrier, inc=1, device_id=dev, device_id_type=MESH)

    for peer in dp_peers:
        greet(peer)

    def greet_chips(k, _):
        greet(chip_peer(k))
        return 0

    lax.fori_loop(1, N_CHIP, greet_chips, 0)
    greet(z_up)
    greet(z_dn)
    greet(partner)
    for load in loads:
        load.start()
    tenant = tid_s[0]
    rank = rank_s[tenant]
    tid_all[g] = jnp.full((1, R), tenant, jnp.int32)

    def remote(src, dst, send, recv, dev):
        return pltpu.make_async_remote_copy(
            src_ref=src, dst_ref=dst, send_sem=send, recv_sem=recv, device_id=dev, device_id_type=MESH
        )

    def arrived(ref, sem):
        remote(ref, ref, s_hop.at[0], sem, partner).wait_recv()

    def sent(ref, sem):
        remote(ref, ref, sem, r_hop.at[0], partner).wait_send()

    pl.semaphore_wait(barrier, n_dp - 1 + N_CHIP - 1 + 3)

    for j, _ in dp_peers:
        rows = a_hbm.at[pl.ds(pl.multiple_of(j // 2 * pr, pr), pr)]
        remote(rows, a_in.at[g], s_hop.at[0], r_hop.at[0], (j, f)).start()
        remote(tid_all.at[g], tid_all.at[g], s_hop.at[5], r_hop.at[5], (j, f)).start()

    def hop1_b():
        for peer in dp_peers:
            remote(bt_hbm, b_in.at[g], s_hop.at[4], r_hop.at[4], peer).start()

    def prepare():
        loads[3].wait()
        masked[...] = jnp.where(row_live, masked[...].astype(F32), 0.0).astype(BF)
        proj_acc[...] = jnp.zeros_like(proj_acc)
        low_acc[...] = jnp.zeros_like(low_acc)

    scale = adapter_alpha_factor / jnp.sqrt(jnp.full((1, R), rank, jnp.int32).astype(F32))
    scale_wide = adapter_alpha_factor / jnp.sqrt(jnp.full((1, VW), rank, jnp.int32).astype(F32))
    rank_live = lax.broadcasted_iota(jnp.int32, (TOK, R), 1) < rank
    row_live = lax.broadcasted_iota(jnp.int32, (TOK, VW), 0) < len_s[0, 0]

    def place(dx, dz):
        return ((x + dx) % NX) * 8 + ((zl + dz) % NZL) * 2 + c

    def rows_at(where, lo, first, last):
        return w.at[pl.ds(pl.multiple_of(where * RW + lo + first, 16), last - first)]

    def w_rows(dx, dz, *span):
        return rows_at(place(dx, dz), *span)

    odd = y % 2
    low_row = (odd * (RW - SIDE), SIDE, (1 - odd) * (RW - SIDE))
    size = (SIDE, RW - 2 * SIDE, SIDE)
    half = (48, 48, 0)

    def span(stream, part):
        lo = low_row[stream]
        ends = {"all": (0, size[stream]), "lo": (0, half[stream]), "hi": (half[stream], size[stream])}[part]
        return lo, ends[0], ends[1]

    def slot(dx, dz):
        return (dx % 4) * 4 + dz % 4

    def w_send(stream, dx, dz, part, axis, step):
        ref = w_rows(dx, dz, *span(stream, part))
        if axis == "x":
            dev = x_up if step == 1 else x_dn
            there = slot(dx - step, dz)
        else:
            dev = z_up if step == 1 else z_dn
            there = slot(dx, dz - step)
        remote(ref, ref, sw_ici, rw_ici.at[stream, there, int(part == "hi")], dev).start()

    def w_d2d(stream, dx, dz, part):
        ref = w_rows(dx, dz, *span(stream, part))
        remote(ref, ref, sw_d2d, rw_d2d.at[stream, slot(dx, dz), int(part == "hi")], partner).start()

    def w_wait(stream, dx, dz, part):
        arrived(w_rows(dx, dz, *span(stream, part)), rw_ici.at[stream, slot(dx, dz), int(part == "hi")])
        w_d2d(stream, dx, dz, part)

    def other_rows(dx, dz, *span):
        return rows_at(place(dx, dz) + 1 - 2 * c, *span)

    def w_other(dx, dz):
        if (dx, dz) == (0, 0):
            arrived(other_rows(0, 0, 0, 0, RW), rw_d2d.at[0, 0, 0])
            return
        for stream in (0, 1, 2):
            for part in parts_of(stream, dx, dz):
                arrived(other_rows(dx, dz, *span(stream, part)), rw_d2d.at[stream, slot(dx, dz), int(part == "hi")])

    def w_side(dx, dz):
        ref = w_rows(dx, dz, *span(0, "all"))
        dev = y_dn if (dx + dz) % 2 else y_up
        remote(ref, ref, sw_ici, rw_ici.at[2, slot(dx, dz), 0], dev).start()

    def w_side_wait(dx, dz):
        arrived(w_rows(dx, dz, *span(2, "all")), rw_ici.at[2, slot(dx, dz), 0])
        w_d2d(2, dx, dz, "all")

    def sides(pairs):
        for dx, dz in pairs:
            w_side_wait(dx, dz)

    def parts_of(stream, dx, dz):
        last = 0
        if stream == 1:
            last = dz if dz else dx
        elif stream == 0:
            last = dx if dx else dz
        return ("lo", "hi") if last == 2 else ("all",)

    def pick(stream, p, q):
        return (p, q) if stream == 1 else (q, p)

    axes = (("z", "x"), ("x", "z"))

    def first_start():
        for stream in (0, 1):
            for step in (1, -1):
                w_send(stream, 0, 0, "all", axes[stream][0], step)
        ref = w_rows(0, 0, 0, 0, RW)
        remote(ref, ref, sw_d2d, rw_d2d.at[0, 0, 0], partner).start()

    def second_start(p):
        for stream in (0, 1):
            for step in (1, -1):
                w_send(stream, *pick(stream, p, 0), "all", axes[stream][1], step)

    def first_wait(p):
        for stream in (0, 1):
            if p == 2:
                for part in ("lo", "hi"):
                    w_wait(stream, *pick(stream, p, 0), part)
                if stream == 0:
                    w_side(*pick(stream, p, 0))
            else:
                w_wait(stream, *pick(stream, p, 0), "all")
                if stream == 0:
                    w_side(*pick(stream, p, 0))
                if p == 3:
                    w_send(stream, *pick(stream, p, 0), "lo", axes[stream][0], 1)
                else:
                    w_send(stream, *pick(stream, p, 0), "hi", axes[stream][0], -1)

    def second_wait(p):
        for stream in (0, 1):
            for q in (3, 1):
                w_wait(stream, *pick(stream, p, q), "all")
                if stream == 0:
                    w_side(*pick(stream, p, q))
                if q == 3:
                    w_send(stream, *pick(stream, p, q), "lo", axes[stream][1], 1)
                else:
                    w_send(stream, *pick(stream, p, q), "hi", axes[stream][1], -1)

    def last_wait(p):
        for stream in (0, 1):
            for part in ("lo", "hi"):
                w_wait(stream, *pick(stream, p, 2), part)
            if stream == 0:
                w_side(*pick(stream, p, 2))

    def choose(k):
        tile = jnp.broadcast_to(tid_all[k], (pr, R))
        total = jnp.zeros((pr, R), F32)
        for u in range(n_dp):
            total = total + jnp.where(tile == u, a_in[u].astype(F32), 0.0)
        return total.astype(BF)

    def z_near(s):
        return (zl, zl + 1 - 2 * (zl % 2), zl + 2 - 4 * (zl // 2), 3 - zl)[s]

    def second_hop():
        arrived(a_in.at[pl.ds(0, n_dp - 1)], r_hop.at[0])
        arrived(tid_all.at[pl.ds(0, n_dp - 1)], r_hop.at[5])
        loads[1].wait()
        mine = a.at[f, pl.ds(pl.multiple_of(y * pr, pr), pr)]

        def send(j, s):
            dev = (j * 2 + zh, x * 8 + z_near(s) * 2 + c)
            remote(q_out.at[j], mine, s_hop.at[1], ra_z.at[s], dev).start()

        def hop2(k, _):
            j = (y + n_y // 2 + (k + 1) // 2 * (2 * (k % 2) - 1)) % n_y
            q_out[j] = choose(j * 2 + zh)
            for s in range(4):
                send(j, s)
            return 0

        lax.fori_loop(0, n_y - 1, hop2, 0)
        q_out[y] = choose(g)
        for s in (1, 2, 3):
            send(y, s)
        a[f, pl.ds(pl.multiple_of(y * pr, pr), pr)] = q_out[y]

    def b_start():
        loads[2].wait()
        arrived(b_in.at[pl.ds(0, n_dp - 1)], r_hop.at[4])
        bt_in[c, chip] = b_in[tenant]
        ref = bt_in.at[c, chip]

        def step(k, _):
            remote(ref, ref, s_hop.at[7], r_hop.at[7], chip_peer(k)).start()
            return 0

        lax.fori_loop(1, N_CHIP, step, 0)

    def b_hand():
        ref = bt_in.at[c]
        arrived(bt_in.at[c, pl.ds(0, N_CHIP - 1)], r_hop.at[7])
        remote(ref, ref, s_hop.at[8], r_hop.at[8], partner).start()

    def b_finish():
        arrived(bt_in.at[1 - c], r_hop.at[8])
        for k in range(N_CHIP):
            for core in (0, 1):
                row = (2 * k + core) * CB
                bt[row : row + CB] = bt_in[core, k]
        glow[...] = jnp.where(rank_live, scale * dot_nn(masked[...], bt[...]), 0.0).astype(BF)

    def a_slot(dx, s):
        return ((x + dx) % NX) * 8 + z_near(s) * 2 + c

    def a_other(dx, s):
        return a_slot(dx, s) + 1 - 2 * c

    def a_d2d(ref, sem):
        remote(ref, ref, sa_d2d, sem, partner).start()

    def a_block_wait(s):
        block = a_slot(0, s)
        ref = a.at[block]
        if s:
            arrived(ref, ra_z.at[s])
        else:
            arrived(a.at[f, pl.ds(0, (n_y - 1) * pr)], ra_z.at[0])
        remote(ref, ref, sa_ici, ra_x.at[s, 0], x_up).start()
        remote(ref, ref, sa_ici, ra_x.at[s, 1], x_dn).start()
        a_d2d(ref, ra_dz.at[s])

    def a_x_wait(s):
        dn = a.at[a_slot(3, s)]
        arrived(dn, ra_x.at[s, 0])
        part = a.at[a_slot(3, s), pl.ds(0, AH)]
        remote(part, part, sa_ici, ra_x.at[s, 2], x_up).start()
        a_d2d(dn, ra_dx.at[s, 0])
        up = a.at[a_slot(1, s)]
        arrived(up, ra_x.at[s, 1])
        part = a.at[a_slot(1, s), pl.ds(AH, AH)]
        remote(part, part, sa_ici, ra_x.at[s, 3], x_dn).start()
        a_d2d(up, ra_dx.at[s, 1])

    def a_x_last(s):
        lo = a.at[a_slot(2, s), pl.ds(0, AH)]
        arrived(lo, ra_x.at[s, 2])
        a_d2d(lo, ra_dx.at[s, 2])
        hi = a.at[a_slot(2, s), pl.ds(AH, AH)]
        arrived(hi, ra_x.at[s, 3])
        a_d2d(hi, ra_dx.at[s, 3])

    def a_other_z(s):
        arrived(a.at[a_other(0, s)], ra_dz.at[s])

    def a_other_x(s):
        arrived(a.at[a_other(3, s)], ra_dx.at[s, 0])
        arrived(a.at[a_other(1, s)], ra_dx.at[s, 1])

    def a_other_last(s):
        arrived(a.at[a_other(2, s), pl.ds(0, AH)], ra_dx.at[s, 2])
        arrived(a.at[a_other(2, s), pl.ds(AH, AH)], ra_dx.at[s, 3])

    def low_of(dx):
        def step(k, _):
            b = (x + dx) % NX * 2 * NZL + k
            low_acc[...] += dot_nn(tok[:, pl.ds(pl.multiple_of(b * RW, RW), RW)], a[b])
            return 0

        lax.fori_loop(0, 2 * NZL, step, 0)

    def cols(p):
        return pl.ds(pl.multiple_of(p * 2 * RW, 2 * RW), 2 * RW)

    def forward(p):
        proj_acc[...] += dot_nn(tok[:, cols(p)], w[cols(p)])

    def backward(p):
        base = dot_nt(masked[...], w[cols(p)])
        low_part = jnp.concatenate([dot_nt(glow[...], a[2 * p + k]) for k in (0, 1)], axis=1)
        gx_ref[:, cols(p)] = (base + low_part).astype(BF)

    def over(pairs, body):
        code_x = sum((dx % 4) * 4**i for i, (dx, dz) in enumerate(pairs))
        code_z = sum((dz % 4) * 4**i for i, (dx, dz) in enumerate(pairs))

        def step(_, carry):
            cx, cz = carry
            body(((x + cx % 4) % NX) * 4 + (zl + cz % 4) % NZL)
            return cx // 4, cz // 4

        lax.fori_loop(0, len(pairs), step, (jnp.int32(code_x), jnp.int32(code_z)))

    def others(pairs):
        for dx, dz in pairs:
            w_other(dx, dz)

    def both(p):
        forward(p)
        backward(p)

    loads[0].wait()
    first_start()
    hop1_b()
    second_start(0)
    prepare()
    first_wait(3)
    first_wait(1)
    second_start(3)
    second_start(1)
    second_hop()
    first_wait(2)
    second_start(2)
    second_wait(0)
    b_start()
    loads[4].wait()
    for s in range(4):
        a_block_wait(s)
    second_wait(3)
    for s in range(4):
        a_other_z(s)
    low_of(0)
    for s in range(4):
        a_x_wait(s)
    for s in range(4):
        a_other_x(s)
    low_of(1)
    low_of(3)
    b_hand()
    for s in range(4):
        a_x_last(s)
    for s in range(4):
        a_other_last(s)
    low_of(2)

    low = jnp.where(rank_live, low_acc[...], 0.0).astype(BF)
    terms = lax.dot_general(masked[...], low, (((0,), (0,)), ((), ())), preferred_element_type=F32) * scale
    terms = terms.reshape(N_CHIP, 2, CB, R)
    rs_out[0] = terms[:, 0]
    rs_out[1] = terms[:, 1]
    core_sum = remote(rs_out.at[1 - c], rs_mid, s_hop.at[2], r_hop.at[2], partner)
    core_sum.start()
    core_sum.wait_recv()
    rs_mid[...] = rs_mid[...] + rs_out[c]
    rs_in[chip] = rs_mid[chip]

    def scatter(k, _):
        remote(rs_mid.at[(chip + k) % N_CHIP], rs_in.at[chip], s_hop.at[6], r_hop.at[6], chip_peer(k)).start()
        return 0

    lax.fori_loop(1, N_CHIP, scatter, 0)

    b_finish()
    proj_acc[...] += scale_wide * dot_nt(low, bt[...])
    second_wait(1)
    second_wait(2)
    near = [(1, 0), (3, 0), (0, 1), (0, 3)]
    sides(near)
    others([(0, 0)] + near)
    over([(0, 0)] + near, both)

    arrived(rs_in.at[pl.ds(0, N_CHIP - 1)], r_hop.at[6])
    total = rs_in[0]
    for k in range(1, N_CHIP):
        total = total + rs_in[k]
    dp_out[...] = total
    dp_in[g] = total

    for peer in dp_peers:
        remote(dp_out, dp_in.at[g], s_hop.at[3], r_hop.at[3], peer).start()

    last_wait(0)
    last_wait(3)
    last_wait(1)
    middle = [(1, 1), (1, 3), (3, 1), (3, 3)]
    sides(middle)
    others(middle)
    over(middle, both)
    last_wait(2)
    late = [(2, 0), (0, 2), (2, 1), (1, 2), (2, 3), (3, 2), (2, 2)]
    sides(late)
    others(late)
    over(late, both)
    proj_ref[...] = jnp.where(row_live, proj_acc[...], 0.0).astype(BF)

    arrived(dp_in.at[pl.ds(0, n_dp - 1)], r_hop.at[3])
    total = jnp.zeros((CB, R), F32)
    for k in range(n_dp):
        total = total + jnp.where(jnp.broadcast_to(tid_all[k], (CB, R)) == g, dp_in[k], 0.0)
    gup_ref[...] = total

    sent(w.at[pl.ds(0, 15 * RW)], sw_ici)
    sent(w.at[pl.ds(0, 16 * RW)], sw_d2d)
    sent(a.at[pl.ds(0, 12)], sa_ici)

    sent(a.at[pl.ds(0, 16)], sa_d2d)
    sent(a_in.at[pl.ds(0, n_dp - 1)], s_hop.at[0])
    sent(a.at[pl.ds(0, 3)], s_hop.at[1])
    sent(a.at[0, pl.ds(0, (n_y - 1) * pr)], s_hop.at[1])
    sent(bt_in.at[0, pl.ds(0, N_CHIP - 1)], s_hop.at[7])
    sent(bt_in.at[0], s_hop.at[8])
    core_sum.wait_send()
    sent(dp_in.at[pl.ds(0, n_dp - 1)], s_hop.at[3])
    sent(b_in.at[pl.ds(0, n_dp - 1)], s_hop.at[4])
    sent(tid_all.at[pl.ds(0, n_dp - 1)], s_hop.at[5])
    sent(rs_in.at[pl.ds(0, N_CHIP - 1)], s_hop.at[6])


def per_device(
    tokens, grad_out, base_weight, frozen_down, trained_up, tenant_per_group, lengths, ranks
):
    n_dp = ranks.shape[0]
    pr = RW // (n_dp // 2)
    hbm = pl.BlockSpec(memory_space=pltpu.HBM)
    smem = pl.BlockSpec(memory_space=pltpu.SMEM)
    vmem = pl.BlockSpec(memory_space=pltpu.VMEM)
    dma = pltpu.SemaphoreType.DMA
    projected, grad_x, up = pl.pallas_call(
        functools.partial(kernel, n_dp),
        out_shape=(
            jax.ShapeDtypeStruct((TOK, VW), BF),
            jax.ShapeDtypeStruct((TOK, N_FSDP * RW), BF),
            jax.ShapeDtypeStruct((CB, R), F32),
        ),
        in_specs=[hbm] * 5 + [smem] * 3,
        out_specs=(vmem, vmem, vmem),
        scratch_shapes=[
            pltpu.VMEM((TOK, N_FSDP * RW), BF),
            pltpu.VMEM((TOK, VW), BF),
            pltpu.VMEM((TOK, R), BF),
            pltpu.VMEM((N_FSDP * RW, VW), BF),
            pltpu.VMEM((N_FSDP, RW, R), BF),
            pltpu.VMEM((n_dp, 1, R), jnp.int32),
            pltpu.VMEM((n_dp, pr, R), BF),
            pltpu.VMEM((n_dp, CB, R), BF),
            pltpu.VMEM((n_dp // 2, pr, R), BF),
            pltpu.VMEM((2, N_CHIP, CB, R), BF),
            pltpu.VMEM((VW, R), BF),
            pltpu.VMEM((2, N_CHIP, CB, R), F32),
            pltpu.VMEM((N_CHIP, CB, R), F32),
            pltpu.VMEM((N_CHIP, CB, R), F32),
            pltpu.VMEM((CB, R), F32),
            pltpu.VMEM((n_dp, CB, R), F32),
            pltpu.VMEM((TOK, VW), F32),
            pltpu.VMEM((TOK, R), F32),
            dma((5,)),
            dma,
            dma,
            dma,
            dma,
            dma((9,)),
            dma((3, 16, 2)),
            dma((3, 16, 2)),
            dma((4,)),
            dma((4, 4)),
            dma((4,)),
            dma((4, 4)),
            dma((9,)),
        ],
        compiler_params=pltpu.CompilerParams(
            collective_id=0, has_side_effects=True, vmem_limit_bytes=40 * 1024 * 1024
        ),
        cost_estimate=pl.CostEstimate(
            flops=2 * 2 * TOK * N_FSDP * RW * (VW + R), bytes_accessed=5 * 1024 * 1024, transcendentals=0
        ),
        name="gather_and_multiply",
    )(
        *[pltpu.with_memory_space_constraint(v, pltpu.HBM) for v in (tokens, grad_out, base_weight, frozen_down[0], jnp.swapaxes(trained_up[0], 0, 1))],
        tenant_per_group, lengths, ranks,
    )
    return projected, grad_x, jnp.swapaxes(up, 0, 1)[None]


def solution(mesh):
    placed = (
        P(("dp", "fsdp"), None),
        P(("dp", "fsdp"), None),
        P("fsdp", None),
        P("dp", "fsdp", None),
        P("dp", None, "fsdp"),
        P("dp"),
        P("dp", "fsdp"),
        P(),
    )
    return jax.shard_map(
        per_device,
        mesh=mesh,
        in_specs=placed,
        out_specs=(P(("dp", "fsdp"), None), P(("dp", "fsdp"), None), P("dp", None, "fsdp")),
        check_vma=False,
    )
```

time: 89.1 us -> 78.6 us (0.88)
  Pallas kernels: 78.7 us -> 73.3 us
  local copies, waits for them, and re-layouts: 8.19 us -> 3.22 us
    pallas_call x1, Pallas kernels: 78.7 us -> 73.3 us  [per_device(): pl.pallas_call(functools.partial(kernel, n_dp), out_shape=(jax.ShapeDtype...]
    unnamed x15 -> x5, local copies, waits for them, and re-layouts: 8.19 us -> 3.22 us
where the time goes in v2:
time: 78.6 us; the launch traced here: 78.4 us
  Pallas kernels  73.3 us (93%)
  local copies, waits for them, and re-layouts  3.22 us (4%)
  between operations  1.94 us (2%)
    pallas_call x1, Pallas kernels, per_device(): pl.pallas_call(functools.partial(kernel, n_dp), out_shape=(jax.ShapeDtype...  73.3 us
    unnamed x5, local copies, waits for them, and re-layouts  3.22 us

profile of v2, /device:TPU:1, one launch (start us, length us, event | category | flops | bytes accessed | tf_op | source)
XLA Modules:
  0.0 78.4 jit_solution(4363645924181292279)
XLA Ops:
  1.9 0.0 copy-start
  1.9 0.6 copy-done
  2.6 73.3 %gather_and_multiply.1 = (bf16[128,512]{1,0:T(8,128)(2,1)S(1)}, bf16[128,8192]{1,0:T(8,128)(2,1)S(1)}, f32[16,128]{1,0:T(8,128)S(1)}) custom-call(bf16[128,8192]{1,0:T(8,128)(2,1)} %tok_hbm.1, bf16[128,512]{1,0:T(8,128)(2,1)} %grad_hbm.1, bf16[256,512]{1,0:T(8,128)(2,1)} %w_hbm.1, bf16[256,128]{1,0:T(8,128)(2,1)} %bitcast.8, bf16[16,128]{1,0:T(8,128)(2,1)} %bitcast.9, ...), custom_call_target="tpu_custom_call" | custom-call | flops 2684354560 | bytes 5242880 | tf_op jit(solution)/shard_map/gather_and_multiply/pallas_call | solution.py:517
  75.8 0.7 copy.16
  76.5 1.3 %copy.17 = bf16[128,8192]{1,0:T(8,128)(2,1)} copy(bf16[128,8192]{1,0:T(8,128)(2,1)S(1)} %get-tuple-element.13) | data formatting | bytes 4194304
  77.8 0.6 copy.18
Async XLA Ops:
  1.9 0.7 copy-start

commit v3 on v2

--- a/solution.py
+++ b/solution.py
@@ -23,7 +23,7 @@
 N_CHIP = N_FSDP // 2
 CB = VW // N_FSDP
 AH = RW // 2
-SIDE = 80
+SIDE = 96
 
 
 def dot_nn(a, b):
@@ -35,9 +35,9 @@
 
 
 def kernel(
-    n_dp, tok_hbm, grad_hbm, w_hbm, a_hbm, bt_hbm, tid_s, len_s, rank_s,
+    n_dp, tok_hbm, grad_hbm, w_hbm, a_hbm, bt_hbm, tid_s, len_s, rank_hbm,
     proj_ref, gx_ref, gup_ref,
-    tok, masked, glow, w, a, tid_all, a_in, b_in, q_out, bt_in, bt, rs_out, rs_mid, rs_in, dp_out, dp_in,
+    rank_s, tok, masked, glow, w, a, tid_all, a_in, b_in, q_out, bt_in, bt, rs_out, rs_mid, rs_in, dp_out, dp_in,
     proj_acc, low_acc,
     load_sem, sw_ici, sw_d2d, sa_ici, sa_d2d, s_hop, rw_ici, rw_d2d, ra_z, ra_x, ra_dz, ra_dx, r_hop,
 ):
@@ -66,6 +66,9 @@
         pltpu.make_async_copy(tok_hbm, tok, load_sem.at[4]),
     ]
 
+    rank_load = pltpu.make_async_copy(rank_hbm, rank_s, load_sem.at[5])
+    rank_load.start()
+
     by_distance = sorted(range(n_y), key=lambda d: -min(d, n_y - d))
     dp_peers = [((y + d) % n_y * 2 + (zh + e) % 2, f) for e in (1, 0) for d in by_distance if d or e]
     chip = f // 2
@@ -92,7 +95,6 @@
     for load in loads:
         load.start()
     tenant = tid_s[0]
-    rank = rank_s[tenant]
     tid_all[g] = jnp.full((1, R), tenant, jnp.int32)
 
     def remote(src, dst, send, recv, dev):
@@ -114,8 +116,14 @@
         remote(tid_all.at[g], tid_all.at[g], s_hop.at[5], r_hop.at[5], (j, f)).start()
 
     def hop1_b():
-        for peer in dp_peers:
-            remote(bt_hbm, b_in.at[g], s_hop.at[4], r_hop.at[4], peer).start()
+        remote(bt_hbm, b_in.at[g], s_hop.at[4], r_hop.at[4], (y * 2 + 1 - zh, f)).start()
+
+    def hop2_b():
+        loads[2].wait()
+        arrived(b_in.at[g], r_hop.at[4])
+        pair = b_in.at[pl.ds(y * 2, 2)]
+        for d in range(1, n_y):
+            remote(pair, pair, s_hop.at[4], r_hop.at[9], ((y + d) % n_y * 2 + zh, f)).start()
 
     def prepare():
         loads[3].wait()
@@ -123,6 +131,8 @@
         proj_acc[...] = jnp.zeros_like(proj_acc)
         low_acc[...] = jnp.zeros_like(low_acc)
 
+    rank_load.wait()
+    rank = rank_s[tenant]
     scale = adapter_alpha_factor / jnp.sqrt(jnp.full((1, R), rank, jnp.int32).astype(F32))
     scale_wide = adapter_alpha_factor / jnp.sqrt(jnp.full((1, VW), rank, jnp.int32).astype(F32))
     rank_live = lax.broadcasted_iota(jnp.int32, (TOK, R), 1) < rank
@@ -140,7 +150,7 @@
     odd = y % 2
     low_row = (odd * (RW - SIDE), SIDE, (1 - odd) * (RW - SIDE))
     size = (SIDE, RW - 2 * SIDE, SIDE)
-    half = (48, 48, 0)
+    half = (48, 32, 0)
 
     def span(stream, part):
         lo = low_row[stream]
@@ -194,16 +204,16 @@
 
     def parts_of(stream, dx, dz):
         last = 0
-        if stream == 1:
+        if stream == 0:
             last = dz if dz else dx
-        elif stream == 0:
+        elif stream == 1:
             last = dx if dx else dz
         return ("lo", "hi") if last == 2 else ("all",)
 
     def pick(stream, p, q):
-        return (p, q) if stream == 1 else (q, p)
-
-    axes = (("z", "x"), ("x", "z"))
+        return (p, q) if stream == 0 else (q, p)
+
+    axes = (("x", "z"), ("z", "x"))
 
     def first_start():
         for stream in (0, 1):
@@ -233,8 +243,8 @@
                 else:
                     w_send(stream, *pick(stream, p, 0), "hi", axes[stream][0], -1)
 
-    def second_wait(p):
-        for stream in (0, 1):
+    def second_wait(p, streams=(0, 1)):
+        for stream in streams:
             for q in (3, 1):
                 w_wait(stream, *pick(stream, p, q), "all")
                 if stream == 0:
@@ -244,8 +254,8 @@
                 else:
                     w_send(stream, *pick(stream, p, q), "hi", axes[stream][1], -1)
 
-    def last_wait(p):
-        for stream in (0, 1):
+    def last_wait(p, streams=(0, 1)):
+        for stream in streams:
             for part in ("lo", "hi"):
                 w_wait(stream, *pick(stream, p, 2), part)
             if stream == 0:
@@ -285,8 +295,7 @@
         a[f, pl.ds(pl.multiple_of(y * pr, pr), pr)] = q_out[y]
 
     def b_start():
-        loads[2].wait()
-        arrived(b_in.at[pl.ds(0, n_dp - 1)], r_hop.at[4])
+        arrived(b_in.at[pl.ds(0, n_dp - 2)], r_hop.at[9])
         bt_in[c, chip] = b_in[tenant]
         ref = bt_in.at[c, chip]
 
@@ -403,11 +412,12 @@
     hop1_b()
     second_start(0)
     prepare()
+    second_hop()
     first_wait(3)
     first_wait(1)
     second_start(3)
     second_start(1)
-    second_hop()
+    hop2_b()
     first_wait(2)
     second_start(2)
     second_wait(0)
@@ -415,16 +425,20 @@
     loads[4].wait()
     for s in range(4):
         a_block_wait(s)
-    second_wait(3)
+    second_wait(3, (0,))
+    second_wait(1, (0,))
     for s in range(4):
         a_other_z(s)
     low_of(0)
     for s in range(4):
         a_x_wait(s)
+    second_wait(2, (0,))
+    second_wait(3, (1,))
     for s in range(4):
         a_other_x(s)
     low_of(1)
     low_of(3)
+    second_wait(1, (1,))
     b_hand()
     for s in range(4):
         a_x_last(s)
@@ -451,12 +465,17 @@
 
     b_finish()
     proj_acc[...] += scale_wide * dot_nt(low, bt[...])
-    second_wait(1)
-    second_wait(2)
+    second_wait(2, (1,))
+    last_wait(0, (0,))
+    last_wait(3, (0,))
+    last_wait(1, (0,))
+    last_wait(2, (0,))
     near = [(1, 0), (3, 0), (0, 1), (0, 3)]
     sides(near)
     others([(0, 0)] + near)
     over([(0, 0)] + near, both)
+    last_wait(0, (1,))
+    last_wait(3, (1,))
 
     arrived(rs_in.at[pl.ds(0, N_CHIP - 1)], r_hop.at[6])
     total = rs_in[0]
@@ -468,18 +487,17 @@
     for peer in dp_peers:
         remote(dp_out, dp_in.at[g], s_hop.at[3], r_hop.at[3], peer).start()
 
-    last_wait(0)
-    last_wait(3)
-    last_wait(1)
-    middle = [(1, 1), (1, 3), (3, 1), (3, 3)]
-    sides(middle)
-    others(middle)
-    over(middle, both)
-    last_wait(2)
-    late = [(2, 0), (0, 2), (2, 1), (1, 2), (2, 3), (3, 2), (2, 2)]
-    sides(late)
-    others(late)
-    over(late, both)
+    def finish(pairs):
+        sides(pairs)
+        others(pairs)
+        over(pairs, both)
+
+    finish([(1, 1), (1, 3), (3, 1), (3, 3)])
+    last_wait(1, (1,))
+    finish([(2, 0), (0, 2)])
+    last_wait(2, (1,))
+    finish([(2, 3), (3, 2), (2, 1), (1, 2)])
+    finish([(2, 2)])
     proj_ref[...] = jnp.where(row_live, proj_acc[...], 0.0).astype(BF)
 
     arrived(dp_in.at[pl.ds(0, n_dp - 1)], r_hop.at[3])
@@ -521,9 +539,10 @@
             jax.ShapeDtypeStruct((TOK, N_FSDP * RW), BF),
             jax.ShapeDtypeStruct((CB, R), F32),
         ),
-        in_specs=[hbm] * 5 + [smem] * 3,
+        in_specs=[hbm] * 5 + [smem, smem, hbm],
         out_specs=(vmem, vmem, vmem),
         scratch_shapes=[
+            pltpu.SMEM((n_dp,), jnp.int32),
             pltpu.VMEM((TOK, N_FSDP * RW), BF),
             pltpu.VMEM((TOK, VW), BF),
             pltpu.VMEM((TOK, R), BF),
@@ -542,19 +561,19 @@
             pltpu.VMEM((n_dp, CB, R), F32),
             pltpu.VMEM((TOK, VW), F32),
             pltpu.VMEM((TOK, R), F32),
-            dma((5,)),
+            dma((6,)),
             dma,
             dma,
             dma,
             dma,
-            dma((9,)),
+            dma((10,)),
             dma((3, 16, 2)),
             dma((3, 16, 2)),
             dma((4,)),
             dma((4, 4)),
             dma((4,)),
             dma((4, 4)),
-            dma((9,)),
+            dma((10,)),
         ],
         compiler_params=pltpu.CompilerParams(
             collective_id=0, has_side_effects=True, vmem_limit_bytes=40 * 1024 * 1024
@@ -564,8 +583,13 @@
         ),
         name="gather_and_multiply",
     )(
-        *[pltpu.with_memory_space_constraint(v, pltpu.HBM) for v in (tokens, grad_out, base_weight, frozen_down[0], jnp.swapaxes(trained_up[0], 0, 1))],
-        tenant_per_group, lengths, ranks,
+        *[
+            pltpu.with_memory_space_constraint(v, pltpu.HBM)
+            for v in (
+                tokens, grad_out, base_weight, frozen_down[0], jnp.swapaxes(trained_up[0], 0, 1)
+            )
+        ],
+        tenant_per_group, lengths, pltpu.with_memory_space_constraint(ranks, pltpu.HBM),
     )
     return projected, grad_x, jnp.swapaxes(up, 0, 1)[None]
 

time: 78.6 us -> 74.5 us (0.948)
  Pallas kernels: 73.3 us -> 69.9 us
    pallas_call x1, Pallas kernels: 73.3 us -> 69.9 us  [per_device(): pl.pallas_call(functools.partial(kernel, n_dp), out_shape=(jax.ShapeDtype...]
    unnamed x5 -> x3, local copies, waits for them, and re-layouts: 3.22 us -> 2.57 us
where the time goes in v3:
time: 74.5 us; the launch traced here: 74.4 us
  Pallas kernels  69.9 us (94%)
  local copies, waits for them, and re-layouts  2.57 us (3%)
  between operations  1.93 us (3%)
    pallas_call x1, Pallas kernels, per_device(): pl.pallas_call(functools.partial(kernel, n_dp), out_shape=(jax.ShapeDtype...  69.9 us
    unnamed x3, local copies, waits for them, and re-layouts  2.57 us

profile of v3, /device:TPU:1, one launch (start us, length us, event | category | flops | bytes accessed | tf_op | source)
XLA Modules:
  0.0 74.4 jit_solution(16636226695453745442)
XLA Ops:
  1.9 69.9 %gather_and_multiply.1 = (bf16[128,512]{1,0:T(8,128)(2,1)S(1)}, bf16[128,8192]{1,0:T(8,128)(2,1)S(1)}, f32[16,128]{1,0:T(8,128)S(1)}) custom-call(bf16[128,8192]{1,0:T(8,128)(2,1)} %tok_hbm.1, bf16[128,512]{1,0:T(8,128)(2,1)} %grad_hbm.1, bf16[256,512]{1,0:T(8,128)(2,1)} %w_hbm.1, bf16[256,128]{1,0:T(8,128)(2,1)} %bitcast.8, bf16[16,128]{1,0:T(8,128)(2,1)} %bitcast.9, ...), custom_call_target="tpu_custom_call" | custom-call | flops 2684354560 | bytes 5242880 | tf_op jit(solution)/shard_map/gather_and_multiply/pallas_call | solution.py:535
  71.8 0.7 copy.16
  72.4 1.3 %copy.17 = bf16[128,8192]{1,0:T(8,128)(2,1)} copy(bf16[128,8192]{1,0:T(8,128)(2,1)S(1)} %get-tuple-element.13) | data formatting | bytes 4194304
  73.8 0.6 copy.18

commit v4 on v3

--- a/solution.py
+++ b/solution.py
@@ -487,17 +487,16 @@
     for peer in dp_peers:
         remote(dp_out, dp_in.at[g], s_hop.at[3], r_hop.at[3], peer).start()
 
-    def finish(pairs):
-        sides(pairs)
-        others(pairs)
-        over(pairs, both)
-
-    finish([(1, 1), (1, 3), (3, 1), (3, 3)])
+    middle = [(1, 1), (1, 3), (3, 1), (3, 3)]
+    late = [(2, 0), (0, 2), (2, 3), (3, 2), (2, 1), (1, 2), (2, 2)]
+    sides(middle)
     last_wait(1, (1,))
-    finish([(2, 0), (0, 2)])
     last_wait(2, (1,))
-    finish([(2, 3), (3, 2), (2, 1), (1, 2)])
-    finish([(2, 2)])
+    sides(late)
+    others(middle)
+    over(middle, both)
+    others(late)
+    over(late, both)
     proj_ref[...] = jnp.where(row_live, proj_acc[...], 0.0).astype(BF)
 
     arrived(dp_in.at[pl.ds(0, n_dp - 1)], r_hop.at[3])

time: 74.5 us -> 72.3 us (0.970)
  Pallas kernels: 69.9 us -> 67.6 us
    pallas_call x1, Pallas kernels: 69.9 us -> 67.6 us  [per_device(): pl.pallas_call(functools.partial(kernel, n_dp), out_shape=(jax.ShapeDtype...]
where the time goes in v4:
time: 72.3 us; the launch traced here: 72.1 us
  Pallas kernels  67.6 us (93%)
  local copies, waits for them, and re-layouts  2.57 us (4%)
  between operations  1.93 us (3%)
    pallas_call x1, Pallas kernels, per_device(): pl.pallas_call(functools.partial(kernel, n_dp), out_shape=(jax.ShapeDtype...  67.6 us
    unnamed x3, local copies, waits for them, and re-layouts  2.57 us

profile of v4, /device:TPU:1, one launch (start us, length us, event | category | flops | bytes accessed | tf_op | source)
XLA Modules:
  0.0 72.1 jit_solution(4247618837357188576)
XLA Ops:
  1.9 67.6 %gather_and_multiply.1 = (bf16[128,512]{1,0:T(8,128)(2,1)S(1)}, bf16[128,8192]{1,0:T(8,128)(2,1)S(1)}, f32[16,128]{1,0:T(8,128)S(1)}) custom-call(bf16[128,8192]{1,0:T(8,128)(2,1)} %tok_hbm.1, bf16[128,512]{1,0:T(8,128)(2,1)} %grad_hbm.1, bf16[256,512]{1,0:T(8,128)(2,1)} %w_hbm.1, bf16[256,128]{1,0:T(8,128)(2,1)} %bitcast.8, bf16[16,128]{1,0:T(8,128)(2,1)} %bitcast.9, ...), custom_call_target="tpu_custom_call" | custom-call | flops 2684354560 | bytes 5242880 | tf_op jit(solution)/shard_map/gather_and_multiply/pallas_call | solution.py:534
  69.6 0.7 copy.16
  70.2 1.3 %copy.17 = bf16[128,8192]{1,0:T(8,128)(2,1)} copy(bf16[128,8192]{1,0:T(8,128)(2,1)S(1)} %get-tuple-element.13) | data formatting | bytes 4194304
  71.5 0.6 copy.18
